TPU v7x, 256 devices: a whole 4x4x8 slice. The times are simulated.
256 devices in a mesh: seq: 32 (over z, x_hi, core), batch: 8 (over x_lo, y).
Axes of the slice: x: 4 (x_hi: 2, x_lo: 2; x = x_hi * 2 + x_lo), y: 4, z: 8, core: 2. Of those that a mesh axis runs over, the one named last changes fastest.
Arguments:
- item_ids: int32 [8, 24576], P('batch', 'seq'), may hold values from 0 to 65535
- table: bfloat16 [65536, 512], P('batch'), may hold values from -6 to 6
- tile_user: int32 [8, 192], P('batch'), may hold values from 0 to 47, never falling along the last dimension, each value on 1 to 19 neighbouring positions
- tail_pad: int32 [8, 48], P('batch'), may hold values from 0 to 127
- w_proj: bfloat16 [512, 2048], replicated, may hold values from -0.25 to 0.25
- w_out: bfloat16 [512, 512], replicated, may hold values from -0.25 to 0.25
Outputs:
- mixed: bfloat16 [8, 24576, 512], P('batch', 'seq')
Inputs may be any that keep to these rules, and one draw needn't show every extreme that they name: `tile_user`: along each group's tiles the user number never falls; every user of the 48 has 1 to 19 tiles and some user exactly 19, so a user's rows lie within 4 neighbouring shards of seq.
All inputs are finite; a program needn't handle non-finite values.
Results may differ from a plain program's by a relative error of at most 0.0059.
Values may be sent and summed in bfloat16 or wider, within the bound.
No kernel may reach another device: no remote copies, remote signals or barrier semaphores. Data moves between devices by JAX's collectives and lax.ppermute only.
A program may use at most 128 MiB of HBM per device.

v0:
```python
import functools

import jax
import jax.numpy as jnp
from jax import lax
from jax.experimental import pallas as pl
from jax.experimental.pallas import tpu as pltpu
from jax.sharding import PartitionSpec as P

HEADS = 8
TILE = 128
REACH = 4
ROOM = 96
SLOTS = 128
MIB = 1 << 20


def vmem():
    return pl.BlockSpec(memory_space=pltpu.VMEM)


def smem():
    return pl.BlockSpec(memory_space=pltpu.SMEM)


def row_norm(values):
    center = values - jnp.mean(values, axis=-1, keepdims=True)
    spread = jnp.mean(center * center, axis=-1, keepdims=True)
    return center * lax.rsqrt(spread + 1e-05)


def half_silu(half):
    return half + half * jnp.tanh(half)


def owner_of(ids, entries, groups):
    owner = jnp.zeros_like(ids)
    for group in range(1, groups):
        owner = owner + jnp.where(ids >= group * entries, 1, 0)
    return owner


def route_kernel(groups, entries, row_ref, list_ref, slot_ref):
    height = row_ref.shape[1]
    ids = row_ref[...]
    lane = lax.broadcasted_iota(jnp.int32, (TILE, height), 1)
    line = lax.broadcasted_iota(jnp.int32, (TILE, height), 0)
    repeat = jnp.zeros((1, height), jnp.int32)
    columns = []
    for start in range(0, height, TILE):
        own_lane = jnp.where(line + start == lane, ids, 0).astype(jnp.float32)
        columns.append(jnp.sum(own_lane, axis=1, keepdims=True).astype(jnp.int32))
        same = (columns[-1] == ids[:, start:]) & (line[:, : height - start] < lane[:, : height - start])
        again = jnp.max(jnp.where(same, 1, 0), axis=0, keepdims=True)
        if start:
            again = jnp.concatenate([jnp.zeros((1, start), jnp.int32), again], axis=1)
        repeat = jnp.maximum(repeat, again)
    fresh = repeat == 0
    owner = owner_of(ids, entries, groups)
    lanes_of = lax.broadcasted_iota(jnp.int32, (groups, height), 0) == owner
    marked = jnp.where(lanes_of & fresh, 1.0, 0.0).astype(jnp.bfloat16)
    rank = jnp.zeros((groups, height), jnp.float32)
    for start in range(0, height, TILE):
        below = jnp.where(line + start < lane, 1.0, 0.0).astype(jnp.bfloat16)
        rank = rank + jnp.dot(
            marked[:, start : start + TILE], below, preferred_element_type=jnp.float32
        )
    place = jnp.sum(jnp.where(lanes_of, rank, 0.0), axis=0, keepdims=True)
    full = jnp.max(jnp.where(fresh, place, 0.0), axis=1, keepdims=True) >= ROOM
    slot = jnp.where(fresh, owner.astype(jnp.float32) * SLOTS + place, 0.0)
    wide = lax.broadcasted_iota(jnp.int32, (TILE, groups * SLOTS), 1)
    wanted = jnp.zeros((1, groups * SLOTS), jnp.int32)
    for start in range(0, height, TILE):
        column = columns[start // TILE]
        mine = jnp.sum(jnp.where(column == ids, slot, 0.0), axis=1, keepdims=True).astype(jnp.int32)
        holder = owner_of(column, entries, groups)
        slot_ref[pl.ds(start, TILE), :] = mine - holder * (SLOTS - ROOM)
        entry = column - holder * entries
        wanted = jnp.maximum(
            wanted, jnp.max(jnp.where(wide == mine, entry, 0), axis=0, keepdims=True)
        )
    place_of = lax.broadcasted_iota(jnp.int32, (1, groups * SLOTS), 1) & (SLOTS - 1)
    list_ref[...] = jnp.where(place_of >= ROOM, jnp.where(full, 1, 0), wanted)


def route(item_ids, groups, entries):
    height = item_ids.shape[1]
    return pl.pallas_call(
        functools.partial(route_kernel, groups, entries),
        out_shape=(
            jax.ShapeDtypeStruct((1, groups * SLOTS), jnp.int32),
            jax.ShapeDtypeStruct((height, 1), jnp.int32),
        ),
        in_specs=[vmem()],
        out_specs=(vmem(), vmem()),
        compiler_params=pltpu.CompilerParams(vmem_limit_bytes=16 * MIB),
        name="route",
    )(item_ids)


def expand_kernel(slot_ref, held_ref, event_ref, normed_ref, head_ref, tail_ref):
    rows = held_ref.shape[0]
    part = TILE
    wide = lax.broadcasted_iota(jnp.int32, (part, rows), 1)

    height = event_ref.shape[0]
    for start in range(0, height, part):
        place = pl.ds(start, part)
        pick = jnp.where(slot_ref[place, :] == wide, 1.0, 0.0).astype(jnp.bfloat16)
        events = jnp.dot(pick, held_ref[...], preferred_element_type=jnp.float32)
        normed = row_norm(events).astype(jnp.bfloat16)
        event_ref[place, :] = events.astype(jnp.bfloat16)
        normed_ref[place, :] = normed
        half_ref = head_ref if start < height // 2 else tail_ref
        half_ref[pl.ds(start % (height // 2), part), :] = normed


def expand(slot, held):
    height, width = slot.shape[0], held.shape[1]
    shape = jax.ShapeDtypeStruct((height, width), jnp.bfloat16)
    part = jax.ShapeDtypeStruct((height // 2, width), jnp.bfloat16)
    return pl.pallas_call(
        expand_kernel,
        out_shape=(shape, shape, part, part),
        in_specs=[vmem(), vmem()],
        out_specs=(vmem(), vmem(), vmem(), vmem()),
        compiler_params=pltpu.CompilerParams(vmem_limit_bytes=16 * MIB),
        name="expand",
    )(slot, held)


def look_up(item_ids, table, w_proj):
    groups = lax.axis_size("batch")
    height = item_ids.shape[1]
    entries, width = table.shape
    wanted, slot = route(item_ids, groups, entries)
    asked = lax.all_to_all(wanted.reshape(groups, SLOTS), "batch", 0, 0, tiled=True)
    crowded = jnp.max(asked[:, ROOM]) > 0
    picked = jnp.take(table, asked[:, :ROOM].reshape(-1), axis=0, mode="clip")
    held = lax.all_to_all(picked, "batch", 0, 0, tiled=True)
    held, w_half = lax.optimization_barrier((held, w_proj * jnp.bfloat16(0.5)))
    found = expand(slot, held)

    def whole():
        every = lax.all_to_all(
            jnp.broadcast_to(item_ids, (groups, height)), "batch", 0, 0, tiled=True
        )
        local = every.reshape(-1) - lax.axis_index("batch") * entries
        dense = jnp.take(table, local, axis=0, mode="clip")
        dense = lax.all_to_all(dense, "batch", 0, 0, tiled=True).reshape(groups, height, width)
        owner = item_ids[0] // entries
        rows = jnp.zeros((height, width), jnp.bfloat16)
        for group in range(groups):
            rows = jnp.where((owner == group)[:, None], dense[group], rows)
        normed = row_norm(rows.astype(jnp.float32)).astype(jnp.bfloat16)
        return rows, normed, normed[: height // 2], normed[height // 2 :]

    return *lax.cond(crowded, whole, lambda: found), w_half


def earlier_tiles(users_ref, tile, most):
    user = users_ref[0, tile]

    def look(back, count):
        at = tile - back
        here = (at >= 0) & (users_ref[0, jnp.maximum(at, 0)] == user)
        return count + jnp.where(here, 1, 0)

    return lax.fori_loop(1, most + 1, look, jnp.int32(0))


def rows_at(tile):
    return pl.ds(pl.multiple_of(tile * TILE, TILE), TILE)


def stack_heads(block, stack_ref, first_tile):
    lane = lax.broadcasted_iota(jnp.int32, (TILE, TILE), 1)
    heads = (lane < TILE // 2, lane >= TILE // 2)
    masks = [jnp.where(head, 1.0, 0.0).astype(jnp.bfloat16) for head in heads]
    for tile in range(block.shape[0] // TILE):
        for at in range(block.shape[1] // TILE):
            both = block[tile * TILE : (tile + 1) * TILE, at * TILE : (at + 1) * TILE]
            for which in range(2):
                place = pl.ds(pl.multiple_of((first_tile + tile) * 2 * TILE, TILE) + which * TILE, TILE)
                stack_ref[at, place, :] = both * masks[which]


def attend(query_ref, key_ref, value_ref, total_ref, rows, places, mask_ref=None, fresh=False):
    for at in range(key_ref.shape[0]):
        columns = slice(at * TILE, (at + 1) * TILE)
        half = lax.dot_general(
            query_ref[rows, columns],
            key_ref[at, places, :],
            (((1,), (1,)), ((), ())),
            preferred_element_type=jnp.float32,
        )
        weights = half_silu(half).astype(jnp.bfloat16)
        if mask_ref is not None:
            weights = weights * mask_ref[...]
        part = jnp.dot(weights, value_ref[at, places, :], preferred_element_type=jnp.float32)
        if fresh:
            total_ref[rows, columns] = part
        else:
            total_ref[rows, columns] += part


def project(normed, proj_ref, at, width):
    half = jnp.dot(
        normed, proj_ref[:, at * width : (at + 1) * width], preferred_element_type=jnp.float32
    )
    return half_silu(half).astype(jnp.bfloat16)


def own_kernel(
    shard_ref,
    users_ref,
    head_ref,
    tail_ref,
    proj_ref,
    gate_ref,
    query_ref,
    total_ref,
    key_ref,
    value_ref,
    mask_ref,
):
    height, width = query_ref.shape
    tiles = height // TILE
    part = height // 2
    base = shard_ref[0, 0] * tiles

    def prepare(half, carry):
        rows = pl.ds(pl.multiple_of(half * part, part), part)
        normed = jnp.where(half == 0, head_ref[...], tail_ref[...])
        gate_ref[rows, :] = project(normed, proj_ref, 0, width)
        query_ref[rows, :] = project(normed, proj_ref, 1, width) * jnp.bfloat16(0.5)
        stack_heads(project(normed, proj_ref, 2, width), key_ref, half * (tiles // 2))
        stack_heads(project(normed, proj_ref, 3, width), value_ref, half * (tiles // 2))
        return carry

    lax.fori_loop(0, 2, prepare, 0)

    line = lax.broadcasted_iota(jnp.int32, (TILE, 2 * part), 0)
    lane = lax.broadcasted_iota(jnp.int32, (TILE, 2 * part), 1)
    key_row = lax.shift_right_logical(lane, 8) * TILE + (lane & (TILE - 1))

    def block(query_half, key_half, fresh):
        def look(tile, carry):
            at = query_half * (tiles // 2) + tile
            first = at - earlier_tiles(users_ref, base + at, tiles - 1)
            least = (first - key_half * (tiles // 2)) * TILE
            most = line + (tile + (query_half - key_half) * (tiles // 2)) * TILE
            seen = (key_row >= least) & (key_row <= most)
            mask_ref[rows_at(tile), :] = jnp.where(seen, 1.0, 0.0).astype(jnp.bfloat16)
            return carry

        lax.fori_loop(0, tiles // 2, look, 0)
        attend(
            query_ref,
            key_ref,
            value_ref,
            total_ref,
            pl.ds(pl.multiple_of(query_half * part, part), part),
            pl.ds(pl.multiple_of(key_half * 2 * part, part), 2 * part),
            mask_ref,
            fresh,
        )

    def same(half, carry):
        block(half, half, True)
        return carry

    lax.fori_loop(0, 2, same, 0)
    middle = base + tiles // 2

    @pl.when(users_ref[0, middle] == users_ref[0, middle - 1])
    def _():
        block(1, 0, False)


def own(shard, users, head, tail, w_proj):
    height, width = 2 * head.shape[0], head.shape[1]
    tiles, pairs = height // TILE, width // TILE
    return pl.pallas_call(
        own_kernel,
        out_shape=(
            jax.ShapeDtypeStruct((height, width), jnp.bfloat16),
            jax.ShapeDtypeStruct((height, width), jnp.bfloat16),
            jax.ShapeDtypeStruct((height, width), jnp.float32),
        ),
        in_specs=[smem(), smem(), vmem(), vmem(), vmem()],
        out_specs=(vmem(), vmem(), vmem()),
        scratch_shapes=[
            pltpu.VMEM((pairs, tiles * 2 * TILE, TILE), jnp.bfloat16),
            pltpu.VMEM((pairs, tiles * 2 * TILE, TILE), jnp.bfloat16),
            pltpu.VMEM((height // 2, height), jnp.bfloat16),
        ],
        compiler_params=pltpu.CompilerParams(vmem_limit_bytes=24 * MIB),
        cost_estimate=pl.CostEstimate(flops=10**6, bytes_accessed=10**5, transcendentals=0),
        name="own",
    )(shard, users, head, tail, w_proj)


def add_half(
    normed, half, begin, asking, proj_ref, query_ref, total_ref, key_ref, value_ref
):
    part, width = normed.shape
    line = lax.broadcasted_iota(jnp.int32, (part, width), 0) + half * part
    values = project(normed, proj_ref, 1, width)
    values = jnp.where(line >= begin, values.astype(jnp.float32), 0.0)
    stack_heads(project(normed, proj_ref, 0, width), key_ref, 0)
    stack_heads(values.astype(jnp.bfloat16), value_ref, 0)

    def query(at, carry):
        attend(
            query_ref,
            key_ref,
            value_ref,
            total_ref,
            pl.ds(pl.multiple_of(at * part, part), part),
            pl.ds(0, 2 * part),
        )
        return carry

    lax.fori_loop(0, jnp.where(asking * TILE > part, 2, 1), query, 0)


def add_earlier(
    block_of, distance, needed, asking, proj_ref, query_ref, total_ref, key_ref, value_ref
):
    height = query_ref.shape[0]
    part = height // 2
    used = used_of(needed, distance, height // TILE)

    @pl.when(used > 0)
    def _():
        total_ref[...] = jnp.zeros_like(total_ref)

    def each(half, carry):
        add_half(
            block_of(half),
            half,
            height - used * TILE,
            asking,
            proj_ref,
            query_ref,
            total_ref,
            key_ref,
            value_ref,
        )
        return carry

    lax.fori_loop(jnp.where(used * TILE > part, 0, 1), jnp.where(used > 0, 2, 0), each, 0)


def used_of(needed, distance, tiles):
    return jnp.clip(needed - tiles * (distance - 1), 0, tiles)


def reach(shard_ref, users_ref, tiles):
    base = shard_ref[0, 0] * tiles
    needed = earlier_tiles(users_ref, base, (REACH - 1) * tiles)
    asking = jnp.int32(0)
    for tile in range(tiles):
        asking = asking + jnp.where(users_ref[0, base + tile] == users_ref[0, base], 1, 0)
    return base, needed, asking


def early_kernel(
    half,
    shard_ref,
    users_ref,
    proj_ref,
    query_ref,
    block_ref,
    total_ref,
    key_ref,
    value_ref,
):
    height = query_ref.shape[0]
    _, needed, asking = reach(shard_ref, users_ref, height // TILE)
    used = used_of(needed, 2, height // TILE)

    @pl.when(used * TILE > height // 2 * (1 - half))
    def _():
        total_ref[...] = jnp.zeros_like(total_ref)
        add_half(
            block_ref[...],
            half,
            height - used * TILE,
            asking,
            proj_ref,
            query_ref,
            total_ref,
            key_ref,
            value_ref,
        )


def middle_kernel(
    shard_ref,
    users_ref,
    proj_ref,
    query_ref,
    block_ref,
    total_ref,
    key_ref,
    value_ref,
):
    part = query_ref.shape[0] // 2

    def block_of(half):
        return block_ref[pl.ds(pl.multiple_of(half * part, part), part), :]

    _, needed, asking = reach(shard_ref, users_ref, query_ref.shape[0] // TILE)
    add_earlier(
        block_of,
        3 - 2 * lax.rem(shard_ref[0, 0], 2),
        needed,
        asking,
        proj_ref,
        query_ref,
        total_ref,
        key_ref,
        value_ref,
    )


def late_kernel(
    shard_ref,
    users_ref,
    pad_ref,
    head_ref,
    tail_ref,
    proj_ref,
    query_ref,
    gate_ref,
    own_ref,
    early_tail_ref,
    early_head_ref,
    middle_ref,
    event_ref,
    out_proj_ref,
    out_ref,
    total_ref,
    key_ref,
    value_ref,
):
    height, width = query_ref.shape
    tiles = height // TILE
    count = users_ref.shape[1]
    base, needed, asking = reach(shard_ref, users_ref, tiles)
    core = lax.rem(shard_ref[0, 0], 2)

    def block_of(half):
        return jnp.where(half == 0, head_ref[...], tail_ref[...])

    add_earlier(
        block_of,
        1 + 2 * core,
        needed,
        asking,
        proj_ref,
        query_ref,
        total_ref,
        key_ref,
        value_ref,
    )
    parts = (
        (early_tail_ref, used_of(needed, 2, tiles)),
        (early_head_ref, used_of(needed, 2, tiles) - tiles // 2),
        (middle_ref, used_of(needed, 3 - 2 * core, tiles)),
        (total_ref, used_of(needed, 1 + 2 * core, tiles)),
    )
    part = height // 2

    line = lax.broadcasted_iota(jnp.int32, (TILE, width), 0)

    def finish(half, carry):
        rows = pl.ds(pl.multiple_of(half * part, part), part)
        inside = lax.broadcasted_iota(jnp.int32, (part, width), 0) + half * part
        attended = own_ref[rows, :]
        for ref, used in parts:
            limit = jnp.where(used > 0, asking * TILE, 0)
            attended = attended + jnp.where(inside < limit, ref[rows, :], 0.0)
        gated = row_norm(attended) * gate_ref[rows, :].astype(jnp.float32)
        mixed = jnp.dot(
            gated.astype(jnp.bfloat16), out_proj_ref[...], preferred_element_type=jnp.float32
        ) + event_ref[rows, :].astype(jnp.float32)
        for tile in range(tiles // 2):
            at = base + half * (tiles // 2) + tile
            here = users_ref[0, at]
            last = (at == count - 1) | (users_ref[0, jnp.minimum(at + 1, count - 1)] != here)
            limit = TILE - jnp.where(last, pad_ref[0, here], 0)
            kept = jnp.where(line < limit, mixed[tile * TILE : (tile + 1) * TILE], 0.0)
            out_ref[rows_at(half * (tiles // 2) + tile), :] = kept.astype(jnp.bfloat16)
        return carry

    lax.fori_loop(0, 2, finish, 0, unroll=True)


def scratch_of(height, width):
    tiles, pairs = height // TILE // 2, width // TILE
    return [
        pltpu.VMEM((pairs, tiles * 2 * TILE, TILE), jnp.bfloat16),
        pltpu.VMEM((pairs, tiles * 2 * TILE, TILE), jnp.bfloat16),
    ]


def earlier_part(kernel, name, flops, shard, users, w_keys_values, queries, *blocks):
    height, width = queries.shape
    return pl.pallas_call(
        kernel,
        out_shape=jax.ShapeDtypeStruct((height, width), jnp.float32),
        in_specs=[smem()] * 2 + [vmem()] * (2 + len(blocks)),
        out_specs=vmem(),
        scratch_shapes=scratch_of(height, width),
        compiler_params=pltpu.CompilerParams(vmem_limit_bytes=24 * MIB),
        cost_estimate=pl.CostEstimate(flops=flops, bytes_accessed=10**5, transcendentals=0),
        name=name,
    )(shard, users, w_keys_values, queries, *blocks)


def late(shard, users, pad, *arrays):
    height, width = arrays[3].shape
    return pl.pallas_call(
        late_kernel,
        out_shape=jax.ShapeDtypeStruct((height, width), jnp.bfloat16),
        in_specs=[smem()] * 3 + [vmem()] * len(arrays),
        out_specs=vmem(),
        scratch_shapes=[pltpu.VMEM((height, width), jnp.float32)] + scratch_of(height, width),
        compiler_params=pltpu.CompilerParams(vmem_limit_bytes=24 * MIB),
        cost_estimate=pl.CostEstimate(
            flops=8 * 10**9, bytes_accessed=10 * 10**6, transcendentals=4 * 10**6
        ),
        name="late",
    )(shard, users, pad, *arrays)


def on_device(item_ids, table, tile_user, tail_pad, w_proj, w_out):
    shards = lax.axis_size("seq")
    shard = lax.axis_index("seq").astype(jnp.int32).reshape(1, 1)
    events, normed, head, tail, w_half = look_up(item_ids, table, w_proj)
    apart = [(i, i + 1 if i % 2 == 0 else i + 3) for i in range(shards)]
    ahead = [(i, i + 2) for i in range(shards - 2)]
    cores = [(i, i ^ 1) for i in range(shards)]
    mid_tail = lax.ppermute(tail, "seq", ahead)
    mid_head = lax.ppermute(head, "seq", ahead)
    apart = [(i, j) for i, j in apart if j < shards]
    odd = lax.ppermute(normed, "seq", apart)
    gate, queries, total = own(shard, tile_user, head, tail, w_half)
    w_keys_values = w_half[:, w_half.shape[1] // 2 :]

    def part_of(kernel, name, flops, *blocks):
        return earlier_part(kernel, name, flops, shard, tile_user, w_keys_values, queries, *blocks)

    mid_tail, queries = lax.optimization_barrier((mid_tail, queries))
    swap_tail = lax.ppermute(mid_tail, "seq", cores)
    early_tail = part_of(functools.partial(early_kernel, 1), "early_tail", 10**6, mid_tail)
    mid_head, early_tail = lax.optimization_barrier((mid_head, early_tail))
    swap_head = lax.ppermute(mid_head, "seq", cores)
    early_head = part_of(functools.partial(early_kernel, 0), "early_head", 5 * 10**9, mid_head)
    odd, early_head = lax.optimization_barrier((odd, early_head))
    middle = part_of(middle_kernel, "middle", 8 * 10**9, odd)
    swap_head, swap_tail, middle = lax.optimization_barrier((swap_head, swap_tail, middle))
    mixed = late(
        shard,
        tile_user,
        tail_pad,
        swap_head,
        swap_tail,
        w_keys_values,
        queries,
        gate,
        total,
        early_tail,
        early_head,
        middle,
        events,
        w_out,
    )
    return mixed[None]


def solution(mesh):
    in_specs = (P("batch", "seq"), P("batch", None), P("batch", None), P("batch", None), P(), P())
    out_specs = P("batch", "seq", None)
    return jax.shard_map(
        on_device, mesh=mesh, in_specs=in_specs, out_specs=out_specs, check_vma=False
    )
```

profile of v0, /device:TPU:105, one launch (start us, length us, event | category | flops | bytes accessed | tf_op | source)
XLA Modules:
  0.0 85.1 jit_solution(9365106948093554181)
XLA Ops:
  0.0 2.3 %route.1 = (s32[1,1024]{1,0:T(1,128)S(1)}, s32[768,1]{1,0:T(8,128)S(1)}) custom-call(s32[1,768]{1,0:T(1,128)} %row_ref.1), custom_call_target="tpu_custom_call" | custom-call | tf_op jit(solution)/shard_map/route/pallas_call | solution.py:88
  2.3 8.9 %all_to_all.36 = s32[8,1,128]{2,1,0:T(1,128)S(1)} all-to-all(s32[8,1,128]{2,1,0:T(1,128)S(1)} %bitcast.68), channel_id=1, replica_groups=mesh['seq'=32,'batch'=8] {'batch'}, dimensions={0} | all-to-all | bytes 8192 | tf_op jit(solution)/shard_map/all_to_all | solution.py:137
  11.2 0.1 reshape.180
  11.2 7.8 %gather_fusion.1 = bf16[768,512]{1,0:T(8,128)(2,1)} fusion(bf16[8192,512]{1,0:T(8,128)(2,1)} %param.9, s32[1024]{0:T(1024)S(1)} %pad_clamp_fusion), kind=kCustom, calls=%fused_computation.1 | custom fusion | bytes 1575936 | tf_op jit(solution)/shard_map/jit(_take)/gather | solution.py:139
  19.1 4.6 %all-to-all-start.3 = ((bf16[8,96,512]{2,1,0:T(8,128)(2,1)}), bf16[8,96,512]{2,1,0:T(8,128)(2,1)S(1)}, u32[]{:S(2)}, u32[]{:S(2)}) async-start(bf16[8,96,512]{2,1,0:T(8,128)(2,1)} %bitcast.14), calls=%async_computation.3 | async-start | bytes 1572864 | tf_op jit(solution)/shard_map/all_to_all | solution.py:140
  23.7 1.8 %broadcast_multiply_fusion.1.proj_ref = bf16[512,2048]{1,0:T(8,128)(2,1)S(1)} fusion(bf16[512,2048]{1,0:T(8,128)(2,1)} %param.12), kind=kLoop, calls=%fused_computation.43 | loop fusion | flops 1048576 | bytes 4194304 | tf_op jit(solution)/shard_map/mul | solution.py:141
  25.5 0.7 slice_reduce_fusion
  26.7 7.5 %all-to-all-done.3 = bf16[8,96,512]{2,1,0:T(8,128)(2,1)S(1)} async-done(((bf16[8,96,512]{2,1,0:T(8,128)(2,1)}), bf16[8,96,512]{2,1,0:T(8,128)(2,1)S(1)}, u32[]{:S(2)}, u32[]{:S(2)}) %all-to-all-start.3) | async-done | bytes 786464 | tf_op jit(solution)/shard_map/all_to_all | solution.py:140
  34.2 2.3 %expand.1 = (bf16[768,512]{1,0:T(8,128)(2,1)}, bf16[768,512]{1,0:T(8,128)(2,1)}, bf16[384,512]{1,0:T(8,128)(2,1)}, bf16[384,512]{1,0:T(8,128)(2,1)}) custom-call(s32[768,1]{1,0:T(8,128)S(1)} %get-tuple-element.40.slot_ref, bf16[768,512]{1,0:T(8,128)(2,1)S(1)} %bitcast.67), custom_call_target="tpu_custom_call" | custom-call | tf_op jit(solution)/shard_map/expand/pallas_call | solution.py:122
  36.6 4.5 %collective-permute-start.1 = (bf16[384,512]{1,0:T(8,128)(2,1)}, bf16[384,512]{1,0:T(8,128)(2,1)S(1)}, u32[]{:S(2)}, u32[]{:S(2)}) collective-permute-start(bf16[384,512]{1,0:T(8,128)(2,1)} %get-tuple-element.44.tail_ref), channel_id=1, source_target_pairs={{0,16},{8,24},{16,32},{24,40},{32,48},{40,56},{48,64},{56,72},{64,... | collective-permute-start | bytes 1179656 | tf_op jit(solution)/shard_map/ppermute | solution.py:547
  41.0 5.0 %collective-permute-start = (bf16[384,512]{1,0:T(8,128)(2,1)}, bf16[384,512]{1,0:T(8,128)(2,1)}, u32[]{:S(2)}, u32[]{:S(2)}) collective-permute-start(bf16[384,512]{1,0:T(8,128)(2,1)} %get-tuple-element.42.head_ref), channel_id=1, source_target_pairs={{0,16},{8,24},{16,32},{24,40},{32,48},{40,56},{48,64},{56,72},{64,... | collective-permute-start | bytes 1179656 | tf_op jit(solution)/shard_map/ppermute | solution.py:548
  46.1 4.6 %collective-permute-start.4 = (bf16[768,512]{1,0:T(8,128)(2,1)}, bf16[768,512]{1,0:T(8,128)(2,1)S(1)}, u32[]{:S(2)}, u32[]{:S(2)}) collective-permute-start(bf16[768,512]{1,0:T(8,128)(2,1)} %get-tuple-element.49), channel_id=1, source_target_pairs={{0,8},{8,32},{16,24},{24,48},{32,40},{40,64},{48,56},{56,80},{64,7... | collective-permute-start | bytes 2359304 | tf_op jit(solution)/shard_map/ppermute | solution.py:550
  50.7 0.0 copy-start.6
  50.7 0.0 copy-start.7
  50.7 0.1 slice.73.proj_ref
  50.8 0.9 %copy-done.6 = bf16[384,512]{1,0:T(8,128)(2,1)S(1)} copy-done((bf16[384,512]{1,0:T(8,128)(2,1)S(1)}, bf16[384,512]{1,0:T(8,128)(2,1)}, u32[]{:S(2)}) %copy-start.6) | copy-done | bytes 393240
  51.7 0.1 copy-done.7
  51.8 8.5 %own.1 = (bf16[768,512]{1,0:T(8,128)(2,1)S(1)}, bf16[768,512]{1,0:T(8,128)(2,1)S(1)}, f32[768,512]{1,0:T(8,128)S(1)}) custom-call(s32[1,1]{1,0:T(1,128)} %bitcast.10.shard_ref, s32[1,192]{1,0:T(1,128)S(1)} %copy-done, bf16[384,512]{1,0:T(8,128)(2,1)S(1)} %copy-done.6, bf16[384,512]{1,0:T(8,128)(2,1)S(1)} %copy-done.7, ...), custom_call_target="tpu_custom_call" | custom-call | flops 1000000 | bytes 100000 | tf_op jit(solution)/shard_map/own/pallas_call | solution.py:284
  60.3 0.0 collective-permute-done.1.block_ref
  60.3 0.1 collective-permute-start.3
  60.4 4.3 %early_tail.1.early_tail_ref = f32[768,512]{1,0:T(8,128)S(1)} custom-call(s32[1,1]{1,0:T(1,128)} %bitcast.10.shard_ref, s32[1,192]{1,0:T(1,128)S(1)} %copy-done, bf16[512,1024]{1,0:T(8,128)(2,1)S(1)} %slice.73.proj_ref, bf16[768,512]{1,0:T(8,128)(2,1)S(1)} %get-tuple-element.46.query_ref, bf16[384,512]{1,0:T(8,128)(2,1)S(1)} %collective-permute-done.1.block_ref), custom_call_target="tpu_custom_call" | custom-call | flops 1000000 | bytes 100000 | tf_op jit(solution)/shard_map/early_tail/pallas_call | solution.py:512
  64.8 0.0 collective-permute-done.block_ref
  64.8 0.6 collective-permute-start.2
  65.4 4.8 %early_head.1.early_head_ref = f32[768,512]{1,0:T(8,128)S(1)} custom-call(s32[1,1]{1,0:T(1,128)} %bitcast.10.shard_ref, s32[1,192]{1,0:T(1,128)S(1)} %copy-done, bf16[512,1024]{1,0:T(8,128)(2,1)S(1)} %slice.73.proj_ref, bf16[768,512]{1,0:T(8,128)(2,1)S(1)} %get-tuple-element.46.query_ref, bf16[384,512]{1,0:T(8,128)(2,1)} %collective-permute-done.block_ref), custom_call_target="tpu_custom_call" | custom-call | flops 5000000000 | bytes 100000 | tf_op jit(solution)/shard_map/early_head/pallas_call | solution.py:512
  70.2 0.0 copy-start.1
  70.2 0.0 copy-start.2
  70.2 0.0 copy-start.4
  70.2 0.0 collective-permute-done.4.block_ref
  70.2 8.1 %middle.1.middle_ref = f32[768,512]{1,0:T(8,128)S(1)} custom-call(s32[1,1]{1,0:T(1,128)} %bitcast.10.shard_ref, s32[1,192]{1,0:T(1,128)S(1)} %copy-done, bf16[512,1024]{1,0:T(8,128)(2,1)S(1)} %slice.73.proj_ref, bf16[768,512]{1,0:T(8,128)(2,1)S(1)} %get-tuple-element.46.query_ref, bf16[768,512]{1,0:T(8,128)(2,1)S(1)} %collective-permute-done.4.block_ref), custom_call_target="tpu_custom_call" | custom-call | flops 8000000000 | bytes 100000 | tf_op jit(solution)/shard_map/middle/pallas_call | solution.py:512
  78.3 0.0 collective-permute-done.2.head_ref
  78.3 0.0 collective-permute-done.3.tail_ref
  78.4 6.7 %late.1 = bf16[768,512]{1,0:T(8,128)(2,1)} custom-call(s32[1,1]{1,0:T(1,128)} %bitcast.10.shard_ref, s32[1,192]{1,0:T(1,128)S(1)} %copy-done, s32[1,48]{1,0:T(1,128)S(1)} %copy-done.2, bf16[384,512]{1,0:T(8,128)(2,1)S(1)} %collective-permute-done.2.head_ref, bf16[384,512]{1,0:T(8,128)(2,1)S(1)} %collective-permute-done.3.tail_ref, ...), custom_call_target="tpu_custom_call" | custom-call | flops 8000000000 | bytes 10000000 | tf_op jit(solution)/shard_map/late/pallas_call | solution.py:526
  (9 shorter events, 0.0 us)
Async XLA Ops:
  19.1 15.2 %all-to-all-start.3 = ((bf16[8,96,512]{2,1,0:T(8,128)(2,1)}), bf16[8,96,512]{2,1,0:T(8,128)(2,1)S(1)}, u32[]{:S(2)}, u32[]{:S(2)}) async-start(bf16[8,96,512]{2,1,0:T(8,128)(2,1)} %bitcast.14), calls=%async_computation.3 | async-start | bytes 1572864 | tf_op jit(solution)/shard_map/all_to_all | solution.py:140
  23.7 10.5 %copy-start.8 = (s32[1,768]{1,0:T(1,128)S(1)}, s32[1,768]{1,0:T(1,128)}, u32[]{:S(2)}) copy-start(s32[1,768]{1,0:T(1,128)} %row_ref.1) | copy-start | bytes 9220
  36.6 14.3 %copy-start = (s32[1,192]{1,0:T(1,128)S(1)}, s32[1,192]{1,0:T(1,128)}, u32[]{:S(2)}) copy-start(s32[1,192]{1,0:T(1,128)} %users_ref.9) | copy-start | bytes 2308
  36.6 23.8 %collective-permute-start.1 = (bf16[384,512]{1,0:T(8,128)(2,1)}, bf16[384,512]{1,0:T(8,128)(2,1)S(1)}, u32[]{:S(2)}, u32[]{:S(2)}) collective-permute-start(bf16[384,512]{1,0:T(8,128)(2,1)} %get-tuple-element.44.tail_ref), channel_id=1, source_target_pairs={{0,16},{8,24},{16,32},{24,40},{32,48},{40,56},{48,64},{56,72},{64,... | collective-permute-start | bytes 1179656 | tf_op jit(solution)/shard_map/ppermute | solution.py:547
  41.0 23.7 %collective-permute-start = (bf16[384,512]{1,0:T(8,128)(2,1)}, bf16[384,512]{1,0:T(8,128)(2,1)}, u32[]{:S(2)}, u32[]{:S(2)}) collective-permute-start(bf16[384,512]{1,0:T(8,128)(2,1)} %get-tuple-element.42.head_ref), channel_id=1, source_target_pairs={{0,16},{8,24},{16,32},{24,40},{32,48},{40,56},{48,64},{56,72},{64,... | collective-permute-start | bytes 1179656 | tf_op jit(solution)/shard_map/ppermute | solution.py:548
  46.1 24.2 %collective-permute-start.4 = (bf16[768,512]{1,0:T(8,128)(2,1)}, bf16[768,512]{1,0:T(8,128)(2,1)S(1)}, u32[]{:S(2)}, u32[]{:S(2)}) collective-permute-start(bf16[768,512]{1,0:T(8,128)(2,1)} %get-tuple-element.49), channel_id=1, source_target_pairs={{0,8},{8,32},{16,24},{24,48},{32,40},{40,64},{48,56},{56,80},{64,7... | collective-permute-start | bytes 2359304 | tf_op jit(solution)/shard_map/ppermute | solution.py:550
  50.7 1.0 %copy-start.6 = (bf16[384,512]{1,0:T(8,128)(2,1)S(1)}, bf16[384,512]{1,0:T(8,128)(2,1)}, u32[]{:S(2)}) copy-start(bf16[384,512]{1,0:T(8,128)(2,1)} %get-tuple-element.42.head_ref) | copy-start | bytes 1179652
  50.7 1.1 %copy-start.7 = (bf16[384,512]{1,0:T(8,128)(2,1)S(1)}, bf16[384,512]{1,0:T(8,128)(2,1)}, u32[]{:S(2)}) copy-start(bf16[384,512]{1,0:T(8,128)(2,1)} %get-tuple-element.44.tail_ref) | copy-start | bytes 1179652
  60.3 18.0 %collective-permute-start.3 = (bf16[384,512]{1,0:T(8,128)(2,1)S(1)}, bf16[384,512]{1,0:T(8,128)(2,1)S(1)}, u32[]{:S(2)}, u32[]{:S(2)}) collective-permute-start(bf16[384,512]{1,0:T(8,128)(2,1)S(1)} %collective-permute-done.1.block_ref), channel_id=1, source_target_pairs={{0,8},{8,0},{16,24},{24,16},{32,40},{40,32},{48,56},{56,48},{64,72... | collective-permute-start | bytes 1179656 | tf_op jit(solution)/shard_map/ppermute | solution.py:558
  64.8 13.5 %collective-permute-start.2 = (bf16[384,512]{1,0:T(8,128)(2,1)}, bf16[384,512]{1,0:T(8,128)(2,1)S(1)}, u32[]{:S(2)}, u32[]{:S(2)}) collective-permute-start(bf16[384,512]{1,0:T(8,128)(2,1)} %collective-permute-done.block_ref), channel_id=1, source_target_pairs={{0,8},{8,0},{16,24},{24,16},{32,40},{40,32},{48,56},{56,48},{64,72... | collective-permute-start | bytes 1179656 | tf_op jit(solution)/shard_map/ppermute | solution.py:561
  70.2 8.2 %copy-start.1 = (bf16[512,512]{1,0:T(8,128)(2,1)S(1)}, bf16[512,512]{1,0:T(8,128)(2,1)}, u32[]{:S(2)}) copy-start(bf16[512,512]{1,0:T(8,128)(2,1)} %out_proj_ref.1) | copy-start | bytes 1572868
  70.2 8.2 %copy-start.2 = (s32[1,48]{1,0:T(1,128)S(1)}, s32[1,48]{1,0:T(1,128)}, u32[]{:S(2)}) copy-start(s32[1,48]{1,0:T(1,128)} %pad_ref.1) | copy-start | bytes 580
  70.2 8.1 %copy-start.4 = (bf16[768,512]{1,0:T(8,128)(2,1)S(1)}, bf16[768,512]{1,0:T(8,128)(2,1)}, u32[]{:S(2)}) copy-start(bf16[768,512]{1,0:T(8,128)(2,1)} %get-tuple-element.58.event_ref) | copy-start | bytes 2359300
where the time goes:
time: 85.6 us; the launch traced here: 85.1 us
  Pallas kernels  37 us (43%)
  starting transfers between devices  19.4 us (23%)
  local copies, waits for them, and re-layouts  9 us (11%)
  blocking collectives  8.91 us (10%)
  waiting for transfers between devices  7.54 us (9%)
  other arithmetic  2.46 us (3%)
    pallas_call x3, Pallas kernels, earlier_part(): pl.pallas_call(kernel, out_shape=jax.ShapeDtypeStruct((height, width), jn...  17.2 us
    all_to_all x1, blocking collectives, look_up(): lax.all_to_all(wanted.reshape(groups, SLOTS), 'batch', 0, 0, tiled=True)  8.91 us
    pallas_call x1, Pallas kernels, own(): pl.pallas_call(own_kernel, out_shape=(jax.ShapeDtypeStruct((height, width...  8.49 us
    gather x1, local copies, waits for them, and re-layouts, look_up(): picked = jnp.take(table, asked[:, :ROOM].reshape(-1), axis=0, mode='clip')  7.82 us
    all_to_all x1, waiting for transfers between devices, look_up(): held = lax.all_to_all(picked, 'batch', 0, 0, tiled=True)  7.53 us
    pallas_call x1, Pallas kernels, late(): pl.pallas_call(late_kernel, out_shape=jax.ShapeDtypeStruct((height, width...  6.7 us
    ppermute x1, starting transfers between devices, on_device(): mid_head = lax.ppermute(head, 'seq', ahead)  5 us
    ppermute x1, starting transfers between devices, on_device(): odd = lax.ppermute(normed, 'seq', apart)  4.64 us
  transfers between devices with their start and end apart: 6, of which 1 were waited for; matrix products, arithmetic and copies ran while one was open for 3% of the time, Pallas kernels for 30%

commit v1 on v0

--- a/solution.py
+++ b/solution.py
@@ -98,7 +98,7 @@
     )(item_ids)
 
 
-def expand_kernel(slot_ref, held_ref, event_ref, normed_ref, head_ref, tail_ref):
+def expand_kernel(slot_ref, held_ref, event_ref, normed_ref, mine_ref, head_ref, tail_ref):
     rows = held_ref.shape[0]
     part = TILE
     wide = lax.broadcasted_iota(jnp.int32, (part, rows), 1)
@@ -111,6 +111,7 @@
         normed = row_norm(events).astype(jnp.bfloat16)
         event_ref[place, :] = events.astype(jnp.bfloat16)
         normed_ref[place, :] = normed
+        mine_ref[place, :] = normed
         half_ref = head_ref if start < height // 2 else tail_ref
         half_ref[pl.ds(start % (height // 2), part), :] = normed
 
@@ -121,9 +122,9 @@
     part = jax.ShapeDtypeStruct((height // 2, width), jnp.bfloat16)
     return pl.pallas_call(
         expand_kernel,
-        out_shape=(shape, shape, part, part),
+        out_shape=(shape, shape, shape, part, part),
         in_specs=[vmem(), vmem()],
-        out_specs=(vmem(), vmem(), vmem(), vmem()),
+        out_specs=(vmem(), vmem(), vmem(), vmem(), vmem()),
         compiler_params=pltpu.CompilerParams(vmem_limit_bytes=16 * MIB),
         name="expand",
     )(slot, held)
@@ -153,7 +154,7 @@
         for group in range(groups):
             rows = jnp.where((owner == group)[:, None], dense[group], rows)
         normed = row_norm(rows.astype(jnp.float32)).astype(jnp.bfloat16)
-        return rows, normed, normed[: height // 2], normed[height // 2 :]
+        return rows, normed, normed, normed[: height // 2], normed[height // 2 :]
 
     return *lax.cond(crowded, whole, lambda: found), w_half
 
@@ -214,8 +215,7 @@
 def own_kernel(
     shard_ref,
     users_ref,
-    head_ref,
-    tail_ref,
+    normed_ref,
     proj_ref,
     gate_ref,
     query_ref,
@@ -231,7 +231,7 @@
 
     def prepare(half, carry):
         rows = pl.ds(pl.multiple_of(half * part, part), part)
-        normed = jnp.where(half == 0, head_ref[...], tail_ref[...])
+        normed = normed_ref[rows, :]
         gate_ref[rows, :] = project(normed, proj_ref, 0, width)
         query_ref[rows, :] = project(normed, proj_ref, 1, width) * jnp.bfloat16(0.5)
         stack_heads(project(normed, proj_ref, 2, width), key_ref, half * (tiles // 2))
@@ -278,8 +278,8 @@
         block(1, 0, False)
 
 
-def own(shard, users, head, tail, w_proj):
-    height, width = 2 * head.shape[0], head.shape[1]
+def own(shard, users, normed, w_proj):
+    height, width = normed.shape
     tiles, pairs = height // TILE, width // TILE
     return pl.pallas_call(
         own_kernel,
@@ -288,7 +288,7 @@
             jax.ShapeDtypeStruct((height, width), jnp.bfloat16),
             jax.ShapeDtypeStruct((height, width), jnp.float32),
         ),
-        in_specs=[smem(), smem(), vmem(), vmem(), vmem()],
+        in_specs=[smem(), smem(), vmem(), vmem()],
         out_specs=(vmem(), vmem(), vmem()),
         scratch_shapes=[
             pltpu.VMEM((pairs, tiles * 2 * TILE, TILE), jnp.bfloat16),
@@ -298,7 +298,7 @@
         compiler_params=pltpu.CompilerParams(vmem_limit_bytes=24 * MIB),
         cost_estimate=pl.CostEstimate(flops=10**6, bytes_accessed=10**5, transcendentals=0),
         name="own",
-    )(shard, users, head, tail, w_proj)
+    )(shard, users, normed, w_proj)
 
 
 def add_half(
@@ -540,7 +540,7 @@
 def on_device(item_ids, table, tile_user, tail_pad, w_proj, w_out):
     shards = lax.axis_size("seq")
     shard = lax.axis_index("seq").astype(jnp.int32).reshape(1, 1)
-    events, normed, head, tail, w_half = look_up(item_ids, table, w_proj)
+    events, normed, mine, head, tail, w_half = look_up(item_ids, table, w_proj)
     apart = [(i, i + 1 if i % 2 == 0 else i + 3) for i in range(shards)]
     ahead = [(i, i + 2) for i in range(shards - 2)]
     cores = [(i, i ^ 1) for i in range(shards)]
@@ -548,7 +548,7 @@
     mid_head = lax.ppermute(head, "seq", ahead)
     apart = [(i, j) for i, j in apart if j < shards]
     odd = lax.ppermute(normed, "seq", apart)
-    gate, queries, total = own(shard, tile_user, head, tail, w_half)
+    gate, queries, total = own(shard, tile_user, mine, w_half)
     w_keys_values = w_half[:, w_half.shape[1] // 2 :]
 
     def part_of(kernel, name, flops, *blocks):

time: 85.6 us -> 85.8 us (level)
  the two profiles are of different devices: /device:TPU:105 before, /device:TPU:131 now
where the time goes in v1:
time: 85.8 us; the launch traced here: 85.1 us
  Pallas kernels  37.2 us (43%)
  starting transfers between devices  17.9 us (21%)
  local copies, waits for them, and re-layouts  9.03 us (11%)
  blocking collectives  8.99 us (10%)
  waiting for transfers between devices  8.67 us (10%)
  other arithmetic  2.52 us (3%)
    pallas_call x3, Pallas kernels, earlier_part(): pl.pallas_call(kernel, out_shape=jax.ShapeDtypeStruct((height, width), jn...  17.2 us
    all_to_all x1, blocking collectives, look_up(): lax.all_to_all(wanted.reshape(groups, SLOTS), 'batch', 0, 0, tiled=True)  8.99 us
    all_to_all x1, waiting for transfers between devices, look_up(): held = lax.all_to_all(picked, 'batch', 0, 0, tiled=True)  8.66 us
    pallas_call x1, Pallas kernels, own(): pl.pallas_call(own_kernel, out_shape=(jax.ShapeDtypeStruct((height, width...  8.52 us
    gather x1, local copies, waits for them, and re-layouts, look_up(): picked = jnp.take(table, asked[:, :ROOM].reshape(-1), axis=0, mode='clip')  7.82 us
    pallas_call x1, Pallas kernels, late(): pl.pallas_call(late_kernel, out_shape=jax.ShapeDtypeStruct((height, width...  6.7 us
    all_to_all x1, starting transfers between devices, look_up(): held = lax.all_to_all(picked, 'batch', 0, 0, tiled=True)  4.65 us
    ppermute x1, starting transfers between devices, on_device(): odd = lax.ppermute(normed, 'seq', apart)  3.96 us
  transfers between devices with their start and end apart: 6, of which 1 were waited for; matrix products, arithmetic and copies ran while one was open for 3% of the time, Pallas kernels for 30%

profile of v1, /device:TPU:131, one launch (start us, length us, event | category | flops | bytes accessed | tf_op | source)
XLA Modules:
  0.0 85.1 jit_solution(5758617774483454469)
XLA Ops:
  0.0 2.3 %route.1 = (s32[1,1024]{1,0:T(1,128)S(1)}, s32[768,1]{1,0:T(8,128)S(1)}) custom-call(s32[1,768]{1,0:T(1,128)} %row_ref.1), custom_call_target="tpu_custom_call" | custom-call | tf_op jit(solution)/shard_map/route/pallas_call | solution.py:88
  2.3 9.0 %all_to_all.36 = s32[8,1,128]{2,1,0:T(1,128)S(1)} all-to-all(s32[8,1,128]{2,1,0:T(1,128)S(1)} %bitcast.68), channel_id=1, replica_groups=mesh['seq'=32,'batch'=8] {'batch'}, dimensions={0} | all-to-all | bytes 8192 | tf_op jit(solution)/shard_map/all_to_all | solution.py:138
  11.3 0.1 reshape.180
  11.3 7.8 %gather_fusion.1 = bf16[768,512]{1,0:T(8,128)(2,1)} fusion(bf16[8192,512]{1,0:T(8,128)(2,1)} %param.9, s32[1024]{0:T(1024)S(1)} %pad_clamp_fusion), kind=kCustom, calls=%fused_computation.1 | custom fusion | bytes 1575936 | tf_op jit(solution)/shard_map/jit(_take)/gather | solution.py:140
  19.2 4.7 %all-to-all-start.3 = ((bf16[8,96,512]{2,1,0:T(8,128)(2,1)}), bf16[8,96,512]{2,1,0:T(8,128)(2,1)S(1)}, u32[]{:S(2)}, u32[]{:S(2)}) async-start(bf16[8,96,512]{2,1,0:T(8,128)(2,1)} %bitcast.14), calls=%async_computation.3 | async-start | bytes 1572864 | tf_op jit(solution)/shard_map/all_to_all | solution.py:141
  23.8 1.8 %broadcast_multiply_fusion.1.proj_ref = bf16[512,2048]{1,0:T(8,128)(2,1)S(1)} fusion(bf16[512,2048]{1,0:T(8,128)(2,1)} %param.12), kind=kLoop, calls=%fused_computation.43 | loop fusion | flops 1048576 | bytes 4194304 | tf_op jit(solution)/shard_map/mul | solution.py:142
  25.6 0.7 slice_reduce_fusion
  27.0 8.7 %all-to-all-done.3 = bf16[8,96,512]{2,1,0:T(8,128)(2,1)S(1)} async-done(((bf16[8,96,512]{2,1,0:T(8,128)(2,1)}), bf16[8,96,512]{2,1,0:T(8,128)(2,1)S(1)}, u32[]{:S(2)}, u32[]{:S(2)}) %all-to-all-start.3) | async-done | bytes 786464 | tf_op jit(solution)/shard_map/all_to_all | solution.py:141
  35.6 0.0 copy-done.7
  35.6 2.5 %expand.1 = (bf16[768,512]{1,0:T(8,128)(2,1)}, bf16[768,512]{1,0:T(8,128)(2,1)}, bf16[768,512]{1,0:T(8,128)(2,1)}, bf16[384,512]{1,0:T(8,128)(2,1)}, bf16[384,512]{1,0:T(8,128)(2,1)}) custom-call(s32[768,1]{1,0:T(8,128)S(1)} %get-tuple-element.43.slot_ref, bf16[768,512]{1,0:T(8,128)(2,1)S(1)} %bitcast.67), custom_call_target="tpu_custom_call" | custom-call | tf_op jit(solution)/shard_map/expand/pallas_call | solution.py:123
  38.1 3.9 %collective-permute-start.1 = (bf16[384,512]{1,0:T(8,128)(2,1)}, bf16[384,512]{1,0:T(8,128)(2,1)S(1)}, u32[]{:S(2)}, u32[]{:S(2)}) collective-permute-start(bf16[384,512]{1,0:T(8,128)(2,1)} %get-tuple-element.47), channel_id=1, source_target_pairs={{0,16},{8,24},{16,32},{24,40},{32,48},{40,56},{48,64},{56,72},{64,... | collective-permute-start | bytes 1179656 | tf_op jit(solution)/shard_map/ppermute | solution.py:547
  42.0 3.5 %collective-permute-start = (bf16[384,512]{1,0:T(8,128)(2,1)}, bf16[384,512]{1,0:T(8,128)(2,1)}, u32[]{:S(2)}, u32[]{:S(2)}) collective-permute-start(bf16[384,512]{1,0:T(8,128)(2,1)} %get-tuple-element.45), channel_id=1, source_target_pairs={{0,16},{8,24},{16,32},{24,40},{32,48},{40,56},{48,64},{56,72},{64,... | collective-permute-start | bytes 1179656 | tf_op jit(solution)/shard_map/ppermute | solution.py:548
  45.5 4.0 %collective-permute-start.4 = (bf16[768,512]{1,0:T(8,128)(2,1)}, bf16[768,512]{1,0:T(8,128)(2,1)S(1)}, u32[]{:S(2)}, u32[]{:S(2)}) collective-permute-start(bf16[768,512]{1,0:T(8,128)(2,1)} %get-tuple-element.53), channel_id=1, source_target_pairs={{0,8},{8,32},{16,24},{24,48},{32,40},{40,64},{48,56},{56,80},{64,7... | collective-permute-start | bytes 2359304 | tf_op jit(solution)/shard_map/ppermute | solution.py:550
  49.4 0.0 copy-start.6
  49.5 0.1 slice.73.proj_ref
  49.6 0.0 copy-done
  49.6 1.0 %copy-done.6 = bf16[768,512]{1,0:T(8,128)(2,1)S(1)} copy-done((bf16[768,512]{1,0:T(8,128)(2,1)S(1)}, bf16[768,512]{1,0:T(8,128)(2,1)}, u32[]{:S(2)}) %copy-start.6) | copy-done | bytes 786456
  50.6 8.5 %own.1 = (bf16[768,512]{1,0:T(8,128)(2,1)S(1)}, bf16[768,512]{1,0:T(8,128)(2,1)S(1)}, f32[768,512]{1,0:T(8,128)S(1)}) custom-call(s32[1,1]{1,0:T(1,128)} %bitcast.10.shard_ref, s32[1,192]{1,0:T(1,128)S(1)} %copy-done, bf16[768,512]{1,0:T(8,128)(2,1)S(1)} %copy-done.6, bf16[512,2048]{1,0:T(8,128)(2,1)S(1)} %broadcast_multiply_fusion.1.proj_ref), custom_call_target="tpu_custom_call" | custom-call | flops 1000000 | bytes 100000 | tf_op jit(solution)/shard_map/own/pallas_call | solution.py:284
  59.1 0.0 collective-permute-done.1.block_ref
  59.1 0.1 collective-permute-start.3
  59.2 4.3 %early_tail.1.early_tail_ref = f32[768,512]{1,0:T(8,128)S(1)} custom-call(s32[1,1]{1,0:T(1,128)} %bitcast.10.shard_ref, s32[1,192]{1,0:T(1,128)S(1)} %copy-done, bf16[512,1024]{1,0:T(8,128)(2,1)S(1)} %slice.73.proj_ref, bf16[768,512]{1,0:T(8,128)(2,1)S(1)} %get-tuple-element.50.query_ref, bf16[384,512]{1,0:T(8,128)(2,1)S(1)} %collective-permute-done.1.block_ref), custom_call_target="tpu_custom_call" | custom-call | flops 1000000 | bytes 100000 | tf_op jit(solution)/shard_map/early_tail/pallas_call | solution.py:512
  63.6 0.0 collective-permute-done.block_ref
  63.6 1.8 %collective-permute-start.2 = (bf16[384,512]{1,0:T(8,128)(2,1)}, bf16[384,512]{1,0:T(8,128)(2,1)S(1)}, u32[]{:S(2)}, u32[]{:S(2)}) collective-permute-start(bf16[384,512]{1,0:T(8,128)(2,1)} %collective-permute-done.block_ref), channel_id=1, source_target_pairs={{0,8},{8,0},{16,24},{24,16},{32,40},{40,32},{48,56},{56,48},{64,72... | collective-permute-start | bytes 1179656 | tf_op jit(solution)/shard_map/ppermute | solution.py:561
  65.4 4.8 %early_head.1.early_head_ref = f32[768,512]{1,0:T(8,128)S(1)} custom-call(s32[1,1]{1,0:T(1,128)} %bitcast.10.shard_ref, s32[1,192]{1,0:T(1,128)S(1)} %copy-done, bf16[512,1024]{1,0:T(8,128)(2,1)S(1)} %slice.73.proj_ref, bf16[768,512]{1,0:T(8,128)(2,1)S(1)} %get-tuple-element.50.query_ref, bf16[384,512]{1,0:T(8,128)(2,1)} %collective-permute-done.block_ref), custom_call_target="tpu_custom_call" | custom-call | flops 5000000000 | bytes 100000 | tf_op jit(solution)/shard_map/early_head/pallas_call | solution.py:512
  70.2 0.0 copy-start.1
  70.2 0.0 copy-start.2
  70.2 0.0 copy-start.5
  70.2 0.0 collective-permute-done.4.block_ref
  70.2 8.1 %middle.1.middle_ref = f32[768,512]{1,0:T(8,128)S(1)} custom-call(s32[1,1]{1,0:T(1,128)} %bitcast.10.shard_ref, s32[1,192]{1,0:T(1,128)S(1)} %copy-done, bf16[512,1024]{1,0:T(8,128)(2,1)S(1)} %slice.73.proj_ref, bf16[768,512]{1,0:T(8,128)(2,1)S(1)} %get-tuple-element.50.query_ref, bf16[768,512]{1,0:T(8,128)(2,1)S(1)} %collective-permute-done.4.block_ref), custom_call_target="tpu_custom_call" | custom-call | flops 8000000000 | bytes 100000 | tf_op jit(solution)/shard_map/middle/pallas_call | solution.py:512
  78.3 0.0 collective-permute-done.2.head_ref
  78.3 0.0 collective-permute-done.3.tail_ref
  78.4 6.7 %late.1 = bf16[768,512]{1,0:T(8,128)(2,1)} custom-call(s32[1,1]{1,0:T(1,128)} %bitcast.10.shard_ref, s32[1,192]{1,0:T(1,128)S(1)} %copy-done, s32[1,48]{1,0:T(1,128)S(1)} %copy-done.2, bf16[384,512]{1,0:T(8,128)(2,1)S(1)} %collective-permute-done.2.head_ref, bf16[384,512]{1,0:T(8,128)(2,1)S(1)} %collective-permute-done.3.tail_ref, ...), custom_call_target="tpu_custom_call" | custom-call | flops 8000000000 | bytes 10000000 | tf_op jit(solution)/shard_map/late/pallas_call | solution.py:526
  (7 shorter events, 0.0 us)
Async XLA Ops:
  19.2 16.5 %all-to-all-start.3 = ((bf16[8,96,512]{2,1,0:T(8,128)(2,1)}), bf16[8,96,512]{2,1,0:T(8,128)(2,1)S(1)}, u32[]{:S(2)}, u32[]{:S(2)}) async-start(bf16[8,96,512]{2,1,0:T(8,128)(2,1)} %bitcast.14), calls=%async_computation.3 | async-start | bytes 1572864 | tf_op jit(solution)/shard_map/all_to_all | solution.py:141
  23.8 11.8 %copy-start.7 = (s32[1,768]{1,0:T(1,128)S(1)}, s32[1,768]{1,0:T(1,128)}, u32[]{:S(2)}) copy-start(s32[1,768]{1,0:T(1,128)} %row_ref.1) | copy-start | bytes 9220
  38.1 11.5 %copy-start = (s32[1,192]{1,0:T(1,128)S(1)}, s32[1,192]{1,0:T(1,128)}, u32[]{:S(2)}) copy-start(s32[1,192]{1,0:T(1,128)} %users_ref.9) | copy-start | bytes 2308
  38.1 21.0 %collective-permute-start.1 = (bf16[384,512]{1,0:T(8,128)(2,1)}, bf16[384,512]{1,0:T(8,128)(2,1)S(1)}, u32[]{:S(2)}, u32[]{:S(2)}) collective-permute-start(bf16[384,512]{1,0:T(8,128)(2,1)} %get-tuple-element.47), channel_id=1, source_target_pairs={{0,16},{8,24},{16,32},{24,40},{32,48},{40,56},{48,64},{56,72},{64,... | collective-permute-start | bytes 1179656 | tf_op jit(solution)/shard_map/ppermute | solution.py:547
  42.0 21.6 %collective-permute-start = (bf16[384,512]{1,0:T(8,128)(2,1)}, bf16[384,512]{1,0:T(8,128)(2,1)}, u32[]{:S(2)}, u32[]{:S(2)}) collective-permute-start(bf16[384,512]{1,0:T(8,128)(2,1)} %get-tuple-element.45), channel_id=1, source_target_pairs={{0,16},{8,24},{16,32},{24,40},{32,48},{40,56},{48,64},{56,72},{64,... | collective-permute-start | bytes 1179656 | tf_op jit(solution)/shard_map/ppermute | solution.py:548
  45.5 24.7 %collective-permute-start.4 = (bf16[768,512]{1,0:T(8,128)(2,1)}, bf16[768,512]{1,0:T(8,128)(2,1)S(1)}, u32[]{:S(2)}, u32[]{:S(2)}) collective-permute-start(bf16[768,512]{1,0:T(8,128)(2,1)} %get-tuple-element.53), channel_id=1, source_target_pairs={{0,8},{8,32},{16,24},{24,48},{32,40},{40,64},{48,56},{56,80},{64,7... | collective-permute-start | bytes 2359304 | tf_op jit(solution)/shard_map/ppermute | solution.py:550
  49.4 1.1 %copy-start.6 = (bf16[768,512]{1,0:T(8,128)(2,1)S(1)}, bf16[768,512]{1,0:T(8,128)(2,1)}, u32[]{:S(2)}) copy-start(bf16[768,512]{1,0:T(8,128)(2,1)} %get-tuple-element.48.normed_ref) | copy-start | bytes 2359300
  59.1 19.2 %collective-permute-start.3 = (bf16[384,512]{1,0:T(8,128)(2,1)S(1)}, bf16[384,512]{1,0:T(8,128)(2,1)S(1)}, u32[]{:S(2)}, u32[]{:S(2)}) collective-permute-start(bf16[384,512]{1,0:T(8,128)(2,1)S(1)} %collective-permute-done.1.block_ref), channel_id=1, source_target_pairs={{0,8},{8,0},{16,24},{24,16},{32,40},{40,32},{48,56},{56,48},{64,72... | collective-permute-start | bytes 1179656 | tf_op jit(solution)/shard_map/ppermute | solution.py:558
  63.6 14.7 %collective-permute-start.2 = (bf16[384,512]{1,0:T(8,128)(2,1)}, bf16[384,512]{1,0:T(8,128)(2,1)S(1)}, u32[]{:S(2)}, u32[]{:S(2)}) collective-permute-start(bf16[384,512]{1,0:T(8,128)(2,1)} %collective-permute-done.block_ref), channel_id=1, source_target_pairs={{0,8},{8,0},{16,24},{24,16},{32,40},{40,32},{48,56},{56,48},{64,72... | collective-permute-start | bytes 1179656 | tf_op jit(solution)/shard_map/ppermute | solution.py:561
  70.2 8.2 %copy-start.1 = (bf16[512,512]{1,0:T(8,128)(2,1)S(1)}, bf16[512,512]{1,0:T(8,128)(2,1)}, u32[]{:S(2)}) copy-start(bf16[512,512]{1,0:T(8,128)(2,1)} %out_proj_ref.1) | copy-start | bytes 1572868
  70.2 8.2 %copy-start.2 = (s32[1,48]{1,0:T(1,128)S(1)}, s32[1,48]{1,0:T(1,128)}, u32[]{:S(2)}) copy-start(s32[1,48]{1,0:T(1,128)} %pad_ref.1) | copy-start | bytes 580
  70.2 8.1 %copy-start.5 = (bf16[768,512]{1,0:T(8,128)(2,1)S(1)}, bf16[768,512]{1,0:T(8,128)(2,1)}, u32[]{:S(2)}) copy-start(bf16[768,512]{1,0:T(8,128)(2,1)} %get-tuple-element.62.event_ref) | copy-start | bytes 2359300
